TPU v7x, 32 devices: a whole 2x2x4 slice. The times are simulated.
32 devices in a mesh: flow: 2 (over x), col: 4 (over y, core), row: 4 (over z).
Axes of the slice: x: 2, y: 2, z: 4, core: 2. Of those that a mesh axis runs over, the one named last changes fastest.
Arguments:
- forcing: float32 [5, 12, 48, 768], P(None, 'flow', 'col', 'row'), may hold values from -6 to 6
- previous: float32 [5, 12, 48, 768], P(None, 'flow', 'col', 'row'), may hold values from -6 to 6
- element_diagonal_shift: float32 [2, 8, 128], P('flow', 'col', 'row'), may hold values from 0.5 to 4
- eigen_bases: float32 [3, 6, 6], replicated, may hold values from -1 to 1, as said below
- eigen_values: float32 [3, 6], replicated, may hold values from 0.5 to 8
- observers: float32 [3, 256], replicated, may hold values from 8 to 30
- panel_points: float32 [3, 1024], P(None, ('flow', 'col', 'row')), may hold values from -2 to 2
- surface_history: float32 [4, 15, 1024], P(None, None, ('flow', 'col', 'row')), may hold values from -6 to 6
Outputs:
- new_state: float32 [5, 12, 48, 768], P(None, 'flow', 'col', 'row')
- spectra: float32 [2, 16, 256], P(None, None, 'row')
Inputs may be any that keep to these rules, and one draw needn't show every extreme that they name: Each eigen_bases[d] is an orthogonal matrix.
All inputs are finite; a program needn't handle non-finite values.
Results may differ from a plain program's by a relative error of at most 0.0003.
Values sent between devices are 32-bit elements; how exact they have to be, the bound alone decides.
A program may use at most 64 MiB of HBM per device.

v0:
```python
import math
import jax
import jax.numpy as jnp
from jax import lax
from jax.sharding import PartitionSpec as P

P_SIZE = 6
SWEEPS = 2
NT = 16
NF = 16
HIGH = lax.Precision.HIGHEST
OMEGA = 0.8
TAU = 0.5
KMAX = 2.0


def with_halo(x, sides, width):
    for axis, dim in sides:
        size, length = (lax.axis_size(axis), x.shape[dim])
        up = [(i, (i + 1) % size) for i in range(size - 1)]
        down = [(j, i) for i, j in up]
        last = lax.slice_in_dim(x, length - width, length, axis=dim)
        first = lax.slice_in_dim(x, 0, width, axis=dim)
        before = lax.ppermute(last, axis, up)
        after = lax.ppermute(first, axis, down)
        x = jnp.concatenate([before, x, after], axis=dim)
    return x


def contract_small(field, matrix, which):
    extent = field.shape
    count = extent[which]
    blocked = field.reshape(extent[:which] + (count // P_SIZE, P_SIZE) + extent[which + 1 :])
    blocked = jnp.moveaxis(blocked, which + 1, -1)
    result = jnp.einsum("...p,qp->...q", blocked, matrix, precision=HIGH)
    result = jnp.moveaxis(result, -1, which + 1)
    return result.reshape(extent)


def contract_last(field, wide_matrix):
    extent = field.shape
    group = wide_matrix.shape[0]
    blocked = field.reshape(extent[0], extent[1], extent[2], extent[3] // group, group)
    result = jnp.einsum("cxybg,hg->cxybh", blocked, wide_matrix, precision=HIGH)
    return result.reshape(extent)


def face_masks(count):
    index = jnp.arange(count) % P_SIZE
    return ((index == P_SIZE - 1).astype(jnp.float32), (index == 0).astype(jnp.float32))


def far_terms(observers, points, source_re, source_im):
    offsets = observers[:, :, None] - points[:, None, :]
    radius = jnp.sqrt(jnp.sum(offsets * offsets, axis=0))
    unit_dir = offsets / radius[None]
    freqs = source_re.shape[1]
    wavenum = (KMAX * (jnp.arange(freqs, dtype=jnp.float32) + 0.5) / freqs)[:, None, None]
    along_re = (
        unit_dir[0][None] * source_re[1][:, None, :]
        + unit_dir[1][None] * source_re[2][:, None, :]
        + unit_dir[2][None] * source_re[3][:, None, :]
    )
    along_im = (
        unit_dir[0][None] * source_im[1][:, None, :]
        + unit_dir[1][None] * source_im[2][:, None, :]
        + unit_dir[2][None] * source_im[3][:, None, :]
    )
    inverse_matrix = 1.0 / radius[None]
    term_re = -wavenum * (source_im[0][:, None, :] + along_im) + along_re * inverse_matrix
    term_im = wavenum * (source_re[0][:, None, :] + along_re) + along_im * inverse_matrix
    phases = wavenum * radius[None]
    amplitude = inverse_matrix / (4.0 * math.pi)
    green_re = amplitude * jnp.cos(phases)
    green_im = -amplitude * jnp.sin(phases)
    total_re = jnp.sum(green_re * term_re - green_im * term_im, axis=2)
    total_im = jnp.sum(green_re * term_im + green_im * term_re, axis=2)
    return jnp.stack([total_re, total_im])


def transform(samples):
    times = jnp.arange(NT, dtype=jnp.float32)
    omegas = math.pi * (jnp.arange(NF, dtype=jnp.float32) + 0.5) / NF
    cos_table = jnp.cos(omegas[:, None] * times[None, :])
    sin_table = jnp.sin(omegas[:, None] * times[None, :])
    source_re = jnp.einsum("fn,cnp->cfp", cos_table, samples, precision=HIGH)
    source_im = -jnp.einsum("fn,cnp->cfp", sin_table, samples, precision=HIGH)
    return (source_re, source_im)


def on_device(
    forcing,
    previous,
    element_diagonal_shift,
    eigen_bases,
    eigen_values,
    observers,
    panel_points,
    surface_history,
):
    extent = forcing.shape
    stiffness = [
        jnp.dot(
            eigen_bases[axis_num] * eigen_values[axis_num][None, :],
            eigen_bases[axis_num].T,
            precision=HIGH,
        )
        for axis_num in range(3)
    ]
    group = P_SIZE * math.gcd(extent[3] // P_SIZE, 64)
    identity = jnp.eye(group // P_SIZE, dtype=jnp.float32)
    wide_stiff = jnp.kron(identity, stiffness[2])
    wide_forward = jnp.kron(identity, eigen_bases[2].T)
    wide_back = jnp.kron(identity, eigen_bases[2])
    shift_nodes = jnp.repeat(
        jnp.repeat(jnp.repeat(element_diagonal_shift, P_SIZE, 0), P_SIZE, 1), P_SIZE, 2
    )
    denominator = (
        shift_nodes
        + jnp.tile(eigen_values[0], extent[1] // P_SIZE)[:, None, None]
        + jnp.tile(eigen_values[1], extent[2] // P_SIZE)[None, :, None]
        + jnp.tile(eigen_values[2], extent[3] // P_SIZE)[None, None, :]
    )
    high_x, low_x = face_masks(extent[1])
    high_y, low_y = face_masks(extent[2])
    high_z, low_z = face_masks(extent[3])
    state = previous
    for sweep in range(SWEEPS):
        apply_result = shift_nodes[None] * state + contract_small(state, stiffness[0], 1)
        apply_result = apply_result + contract_small(state, stiffness[1], 2)
        padded = with_halo(state, (("flow", 1), ("col", 2), ("row", 3)), 1)
        next_x = padded[:, 2:, 1:-1, 1:-1]
        prev_x = padded[:, :-2, 1:-1, 1:-1]
        next_y = padded[:, 1:-1, 2:, 1:-1]
        prev_y = padded[:, 1:-1, :-2, 1:-1]
        next_z = padded[:, 1:-1, 1:-1, 2:]
        prev_z = padded[:, 1:-1, 1:-1, :-2]
        result = high_x[None, :, None, None] * next_x + low_x[None, :, None, None] * prev_x
        result = result + high_y[None, None, :, None] * next_y + low_y[None, None, :, None] * prev_y
        residual = (
            forcing
            - (apply_result + contract_last(state, wide_stiff))
            + TAU
            * (result + high_z[None, None, None, :] * next_z + low_z[None, None, None, :] * prev_z)
        )
        block_result = contract_small(residual, eigen_bases[0].T, 1)
        block_result = contract_small(block_result, eigen_bases[1].T, 2)
        block_result = contract_last(block_result, wide_forward) / denominator[None]
        block_result = contract_small(block_result, eigen_bases[0], 1)
        block_result = contract_small(block_result, eigen_bases[1], 2)
        state = state + OMEGA * contract_last(block_result, wide_back)
    own_panels = panel_points.shape[1]
    newest = state[:4, 0, 0, :own_panels]
    surface_samples = jnp.concatenate([surface_history, newest[:, None, :]], axis=1)
    rows = lax.axis_size("row")
    count = observers.shape[1] // rows
    points, samples = (
        lax.all_gather(panel_points, "row", axis=1, tiled=True),
        lax.all_gather(surface_samples, "row", axis=2, tiled=True),
    )
    source_re, source_im = transform(samples)
    own_obs = lax.dynamic_slice_in_dim(observers, lax.axis_index("row") * count, count, 1)
    partial_sums = far_terms(own_obs, points, source_re, source_im)
    spectra = lax.psum(partial_sums, ("flow", "col"))
    return (state, spectra)


def solution(mesh):
    return jax.shard_map(
        on_device,
        mesh=mesh,
        in_specs=(
            P(None, "flow", "col", "row"),
            P(None, "flow", "col", "row"),
            P("flow", "col", "row"),
            P(),
            P(),
            P(),
            P(None, ("flow", "col", "row")),
            P(None, None, ("flow", "col", "row")),
        ),
        out_specs=(P(None, "flow", "col", "row"), P(None, None, "row")),
        check_vma=False,
    )
```

profile of v0, /device:TPU:0, one launch (start us, length us, event | category | flops | bytes accessed | tf_op | source)
XLA Modules:
  0.0 143.8 jit_solution(3606890502460777156)
XLA Ops:
  0.6 0.9 fusion.168
  1.7 1.3 collective-permute-start
  3.0 4.8 %collective-permute-start.1 = (f32[5,1,12,192]{3,1,2,0:T(1,128)S(1)}, f32[5,1,12,192]{3,1,2,0:T(1,128)S(1)}, u32[]{:S(2)}, u32[]{:S(2)}) collective-permute-start(f32[5,1,12,192]{3,1,2,0:T(1,128)S(1)} %copy.139), channel_id=1, source_target_pairs={{0,16},{1,17},{2,18},{3,19},{4,20},{5,21},{6,22},{7,23},{8,24},{9,... | collective-permute-start | bytes 138248 | tf_op jit(solution)/shard_map/ppermute | solution.py:24
  7.9 1.3 copy.153
  10.8 0.9 fusion.131
  11.7 4.9 %broadcast_multiply_fusion = (f32[32,6,32,6]{3,2,1,0:T(8,128)}, f32[32,6,32,6]{3,2,1,0:T(8,128)}, f32[32,6,32,6]{3,2,1,0:T(8,128)}) fusion(f32[6,6]{1,0:T(8,128)S(1)} %get-tuple-element.42, f32[32,32]{1,0:T(8,128)S(1)} %fusion.118, f32[6,6]{1,0:T(8,128)S(1)} %copy.146, f32[6,6]{1,0:T(8,128)S(1)} %fusion.131), kind=kLoop, calls=%fused_computation | loop fusion | flops 110592 | bytes 446896 | tf_op jit(solution)/shard_map/jit(kron)/mul | solution.py:114
  16.6 3.9 %reshape.301 = f32[192,192,1,1]{1,0,2,3:T(8,128)S(1)} reshape(f32[32,6,32,6]{3,2,1,0:T(8,128)} %get-tuple-element.41) | data formatting | bytes 294912 | tf_op jit(solution)/shard_map/jit(kron)/mul | solution.py:112
  22.9 13.2 %all-gather = f32[4,32,3]{1,2,0:T(4,128)S(1)} all-gather(f32[1,32,3]{1,2,0:T(4,128)S(1)} %bitcast.282), channel_id=1, replica_groups=mesh['flow'=2,'col'=4,'row'=4] {'row'}, dimensions={0}, use_global_device_ids=true | all-gather | bytes 1920 | tf_op jit(solution)/shard_map/all_gather | solution.py:158
  38.5 1.1 fusion.3
  39.7 1.3 collective-permute-start.2
  41.0 3.0 %collective-permute-start.3 = (f32[5,8,1,192]{3,1,2,0:T(8,128)S(1)}, f32[5,8,1,192]{3,1,2,0:T(8,128)S(1)}, u32[]{:S(2)}, u32[]{:S(2)}) collective-permute-start(f32[5,8,1,192]{3,1,2,0:T(8,128)S(1)} %get-tuple-element.14), channel_id=1, source_target_pairs={{0,4},{4,8},{8,12},{1,5},{5,9},{9,13},{2,6},{6,10},{10,14},{3,7},{... | collective-permute-start | bytes 92168 | tf_op jit(solution)/shard_map/ppermute | solution.py:24
  44.1 0.8 collective-permute-done.3
  45.3 4.2 %collective-permute-start.5 = (f32[5,8,14,1]{3,1,2,0:T(8,128)S(1)}, f32[5,8,14,1]{3,1,2,0:T(8,128)}, u32[]{:S(2)}, u32[]{:S(2)}) collective-permute-start(f32[5,8,14,1]{3,1,2,0:T(8,128)S(1)} %get-tuple-element.19), channel_id=1, source_target_pairs={{0,1},{1,2},{2,3},{4,5},{5,6},{6,7},{8,9},{9,10},{10,11},{12,13},{... | collective-permute-start | bytes 6728 | tf_op jit(solution)/shard_map/ppermute | solution.py:24
  49.5 1.5 %collective-permute-start.4 = (f32[5,8,14,1]{3,1,2,0:T(8,128)S(1)}, f32[5,8,14,1]{3,1,2,0:T(8,128)}, u32[]{:S(2)}, u32[]{:S(2)}) collective-permute-start(f32[5,8,14,1]{3,1,2,0:T(8,128)S(1)} %get-tuple-element.18), channel_id=1, source_target_pairs={{1,0},{2,1},{3,2},{5,4},{6,5},{7,6},{9,8},{10,9},{11,10},{13,12},{... | collective-permute-start | bytes 6728 | tf_op jit(solution)/shard_map/ppermute | solution.py:25
  51.0 3.9 %reshape.304 = f32[192,192,1,1]{1,0,2,3:T(8,128)S(1)} reshape(f32[32,6,32,6]{3,2,1,0:T(8,128)} %get-tuple-element.40) | data formatting | bytes 294912 | tf_op jit(solution)/shard_map/jit(kron)/mul | solution.py:113
  54.8 3.9 %reshape.307 = f32[192,192,1,1]{1,0,2,3:T(8,128)S(1)} reshape(f32[32,6,32,6]{3,2,1,0:T(8,128)} %get-tuple-element.39) | data formatting | bytes 294912 | tf_op jit(solution)/shard_map/jit(kron)/mul | solution.py:114
  58.8 2.2 %collective-permute-done.4 = f32[5,8,14,1]{3,1,2,0:T(8,128)} collective-permute-done((f32[5,8,14,1]{3,1,2,0:T(8,128)S(1)}, f32[5,8,14,1]{3,1,2,0:T(8,128)}, u32[]{:S(2)}, u32[]{:S(2)}) %collective-permute-start.4) | collective-permute-done | bytes 2272 | tf_op jit(solution)/shard_map/ppermute | solution.py:25
  61.0 2.7 %fusion.55 = f32[5,12,192,6]{2,3,1,0:T(8,128)S(1)} fusion(f32[5,6,12,192]{3,1,2,0:T(8,128)S(1)} %fusion.3, f32[5,8,14,1]{3,1,2,0:T(8,128)} %collective-permute-done.5, f32[5,8,1,192]{3,1,2,0:T(8,128)S(1)} %collective-permute-done.2, f32[5,8,1,192]{3,1,2,0:T(8,128)S(1)} %collective-permute-done.3, f32[5,1,12,192]{3,1,2,0:T(1,128)S(1)} %collective-permute-done, ...), kind=kOutput, calls=%fused_computation.96 | convolution fusion | flops 7119360 | bytes 1476992 | tf_op jit(solution)/shard_map/...p,qp->...q/dot_general | solution.py:35
  67.9 1.3 collective-permute-start.6
  69.2 4.5 %collective-permute-start.7 = (f32[5,1,12,192]{3,1,2,0:T(1,128)S(1)}, f32[5,1,12,192]{3,1,2,0:T(1,128)S(1)}, u32[]{:S(2)}, u32[]{:S(2)}) collective-permute-start(f32[5,1,12,192]{3,1,2,0:T(1,128)S(1)} %get-tuple-element.20), channel_id=1, source_target_pairs={{0,16},{1,17},{2,18},{3,19},{4,20},{5,21},{6,22},{7,23},{8,24},{9,... | collective-permute-start | bytes 138248 | tf_op jit(solution)/shard_map/ppermute | solution.py:24
  74.4 1.2 collective-permute-done.7
  75.6 1.3 collective-permute-start.8
  76.9 3.3 %collective-permute-start.9 = (f32[5,8,1,192]{3,1,2,0:T(8,128)S(1)}, f32[5,8,1,192]{3,1,2,0:T(8,128)S(1)}, u32[]{:S(2)}, u32[]{:S(2)}) collective-permute-start(f32[5,8,1,192]{3,1,2,0:T(8,128)S(1)} %get-tuple-element.12), channel_id=1, source_target_pairs={{0,4},{4,8},{8,12},{1,5},{5,9},{9,13},{2,6},{6,10},{10,14},{3,7},{... | collective-permute-start | bytes 92168 | tf_op jit(solution)/shard_map/ppermute | solution.py:24
  81.4 2.4 %collective-permute-start.11 = (f32[5,8,14,1]{3,1,2,0:T(8,128)S(1)}, f32[5,8,14,1]{3,1,2,0:T(8,128)S(1)}, u32[]{:S(2)}, u32[]{:S(2)}) collective-permute-start(f32[5,8,14,1]{3,1,2,0:T(8,128)S(1)} %get-tuple-element.17), channel_id=1, source_target_pairs={{0,1},{1,2},{2,3},{4,5},{5,6},{6,7},{8,9},{9,10},{10,11},{12,13},{... | collective-permute-start | bytes 6728 | tf_op jit(solution)/shard_map/ppermute | solution.py:24
  83.8 1.3 collective-permute-start.10
  85.9 2.9 %collective-permute-done.11 = f32[5,8,14,1]{3,1,2,0:T(8,128)S(1)} collective-permute-done((f32[5,8,14,1]{3,1,2,0:T(8,128)S(1)}, f32[5,8,14,1]{3,1,2,0:T(8,128)S(1)}, u32[]{:S(2)}, u32[]{:S(2)}) %collective-permute-start.11) | collective-permute-done | bytes 2272 | tf_op jit(solution)/shard_map/ppermute | solution.py:24
  88.8 4.7 %collective-permute-done.10 = f32[5,8,14,1]{3,1,2,0:T(8,128)S(1)} collective-permute-done((f32[5,8,14,1]{3,1,2,0:T(8,128)S(1)}, f32[5,8,14,1]{3,1,2,0:T(8,128)S(1)}, u32[]{:S(2)}, u32[]{:S(2)}) %collective-permute-start.10) | collective-permute-done | bytes 2272 | tf_op jit(solution)/shard_map/ppermute | solution.py:25
  93.5 1.7 %fusion.28 = f32[5,12,192,6]{2,3,1,0:T(8,128)S(1)} fusion(f32[5,6,12,192]{3,1,2,0:T(8,128)S(1)} %fusion.7, f32[5,8,14,1]{3,1,2,0:T(8,128)S(1)} %collective-permute-done.11, f32[5,8,1,192]{3,1,2,0:T(8,128)S(1)} %collective-permute-done.8, f32[5,8,1,192]{3,1,2,0:T(8,128)S(1)} %collective-permute-done.9, f32[5,1,12,192]{3,1,2,0:T(1,128)S(1)} %collective-permute-done.6, ...), kind=kOutput, calls=%fused_computation.57 | convolution fusion | flops 7119360 | bytes 2045952 | tf_op jit(solution)/shard_map/...p,qp->...q/dot_general | solution.py:35
  99.0 0.9 copy.174
  100.2 14.4 %all_gather.7 = f32[4,16,128]{1,0,2:T(4,128)S(1)} all-gather(f32[4,16,32]{1,0,2:T(4,128)S(1)} %pad_maximum_fusion.62), channel_id=1, replica_groups=mesh['flow'=2,'col'=4,'row'=4] {'row'}, dimensions={2}, use_global_device_ids=true | all-gather | bytes 40960 | tf_op jit(solution)/shard_map/all_gather | solution.py:159
  115.4 2.7 %fusion.17 = (f32[16,64]{1,0:T(8,128)S(1)}, f32[16,64]{1,0:T(8,128)S(1)}) fusion(f32[16,128]{1,0:T(8,128)S(1)} %get-tuple-element.36, f32[64,128]{1,0:T(8,128)S(1)} %copy-done.6, f32[64,128]{1,0:T(8,128)S(1)} %copy-done.7, f32[16,128]{1,0:T(8,128)S(1)} %get-tuple-element.37, f32[16,128]{1,0:T(8,128)S(1)} %get-tuple-element.38, ...), kind=kLoop, calls=%fused_computation.41 | loop fusion | flops 3799040 | bytes 303232 | tf_op jit(solution)/shard_map/reduce_sum | solution.py:76
  118.1 25.7 %psum.7 = f32[2,16,64]{2,1,0:T(8,128)} all-reduce(f32[2,16,64]{2,1,0:T(8,128)S(1)} %pad_maximum_fusion.69), channel_id=1, replica_groups=mesh['flow'=2,'col'=4,'row'=4] {'flow','col'}, use_global_device_ids=true, to_apply=%region_3.4 | all-reduce | flops 2048 | bytes 16384 | tf_op jit(solution)/shard_map/psum | solution.py:164
  (102 shorter events, 18.2 us)
Async XLA Ops:
  0.6 35.6 %copy-start = (f32[3,256]{1,0:T(4,128)S(1)}, f32[3,256]{1,0:T(4,128)}, u32[]{:S(2)}) copy-start(f32[3,256]{1,0:T(4,128)} %param.13) | copy-start | bytes 9220
  1.7 38.0 %collective-permute-start = (f32[5,1,12,192]{3,1,2,0:T(1,128)S(1)}, f32[5,1,12,192]{3,1,2,0:T(1,128)S(1)}, u32[]{:S(2)}, u32[]{:S(2)}) collective-permute-start(f32[5,1,12,192]{3,1,2,0:T(1,128)S(1)} %copy.137), channel_id=1, source_target_pairs={{16,0},{17,1},{18,2},{19,3},{20,4},{21,5},{22,6},{23,7},{24,8},{25... | collective-permute-start | bytes 138248 | tf_op jit(solution)/shard_map/ppermute | solution.py:25
  3.0 36.6 %collective-permute-start.1 = (f32[5,1,12,192]{3,1,2,0:T(1,128)S(1)}, f32[5,1,12,192]{3,1,2,0:T(1,128)S(1)}, u32[]{:S(2)}, u32[]{:S(2)}) collective-permute-start(f32[5,1,12,192]{3,1,2,0:T(1,128)S(1)} %copy.139), channel_id=1, source_target_pairs={{0,16},{1,17},{2,18},{3,19},{4,20},{5,21},{6,22},{7,23},{8,24},{9,... | collective-permute-start | bytes 138248 | tf_op jit(solution)/shard_map/ppermute | solution.py:24
  16.6 4.0 %copy-start.1 = (f32[5,6,12,192]{3,2,1,0:T(8,128)S(1)}, f32[5,6,12,192]{3,2,1,0:T(8,128)}, u32[]{:S(2)}) copy-start(f32[5,6,12,192]{3,2,1,0:T(8,128)} %param.9) | copy-start | bytes 829444
  16.6 4.7 %copy-start.3 = (f32[3,6,6]{2,1,0:T(8,128)S(1)}, f32[3,6,6]{2,1,0:T(8,128)}, u32[]{:S(2)}) copy-start(f32[3,6,6]{2,1,0:T(8,128)} %param.11) | copy-start | bytes 1300
  16.6 5.8 %copy-start.13 = (f32[1,2,32]{2,1,0:T(2,128)S(1)}, f32[1,2,32]{2,1,0:T(2,128)}, u32[]{:S(2)}) copy-start(f32[1,2,32]{2,1,0:T(2,128)} %param.10) | copy-start | bytes 772
  16.6 6.3 %copy-start.12 = (f32[3,32]{1,0:T(4,128)S(1)}, f32[3,32]{1,0:T(4,128)}, u32[]{:S(2)}) copy-start(f32[3,32]{1,0:T(4,128)} %param.14) | copy-start | bytes 1156
  16.6 21.9 %copy-start.2 = (f32[5,6,12,192]{3,2,1,0:T(8,128)S(1)}, f32[5,6,12,192]{3,2,1,0:T(8,128)}, u32[]{:S(2)}) copy-start(f32[5,6,12,192]{3,2,1,0:T(8,128)} %param.8) | copy-start | bytes 829444
  39.7 4.4 %collective-permute-start.2 = (f32[5,8,1,192]{3,1,2,0:T(8,128)S(1)}, f32[5,8,1,192]{3,1,2,0:T(8,128)S(1)}, u32[]{:S(2)}, u32[]{:S(2)}) collective-permute-start(f32[5,8,1,192]{3,1,2,0:T(8,128)S(1)} %get-tuple-element.15), channel_id=1, source_target_pairs={{4,0},{8,4},{12,8},{5,1},{9,5},{13,9},{6,2},{10,6},{14,10},{7,3},{... | collective-permute-start | bytes 92168 | tf_op jit(solution)/shard_map/ppermute | solution.py:25
  41.0 3.9 %collective-permute-start.3 = (f32[5,8,1,192]{3,1,2,0:T(8,128)S(1)}, f32[5,8,1,192]{3,1,2,0:T(8,128)S(1)}, u32[]{:S(2)}, u32[]{:S(2)}) collective-permute-start(f32[5,8,1,192]{3,1,2,0:T(8,128)S(1)} %get-tuple-element.14), channel_id=1, source_target_pairs={{0,4},{4,8},{8,12},{1,5},{5,9},{9,13},{2,6},{6,10},{10,14},{3,7},{... | collective-permute-start | bytes 92168 | tf_op jit(solution)/shard_map/ppermute | solution.py:24
  45.3 13.6 %collective-permute-start.5 = (f32[5,8,14,1]{3,1,2,0:T(8,128)S(1)}, f32[5,8,14,1]{3,1,2,0:T(8,128)}, u32[]{:S(2)}, u32[]{:S(2)}) collective-permute-start(f32[5,8,14,1]{3,1,2,0:T(8,128)S(1)} %get-tuple-element.19), channel_id=1, source_target_pairs={{0,1},{1,2},{2,3},{4,5},{5,6},{6,7},{8,9},{9,10},{10,11},{12,13},{... | collective-permute-start | bytes 6728 | tf_op jit(solution)/shard_map/ppermute | solution.py:24
  49.5 11.6 %collective-permute-start.4 = (f32[5,8,14,1]{3,1,2,0:T(8,128)S(1)}, f32[5,8,14,1]{3,1,2,0:T(8,128)}, u32[]{:S(2)}, u32[]{:S(2)}) collective-permute-start(f32[5,8,14,1]{3,1,2,0:T(8,128)S(1)} %get-tuple-element.18), channel_id=1, source_target_pairs={{1,0},{2,1},{3,2},{5,4},{6,5},{7,6},{9,8},{10,9},{11,10},{13,12},{... | collective-permute-start | bytes 6728 | tf_op jit(solution)/shard_map/ppermute | solution.py:25
  51.0 7.7 %copy-start.11 = (f32[4,15,32]{2,0,1:T(4,128)S(1)}, f32[4,15,32]{2,0,1:T(4,128)}, u32[]{:S(2)}) copy-start(f32[4,15,32]{2,0,1:T(4,128)} %param.15) | copy-start | bytes 23044
  61.0 3.6 %copy-start.4 = (f32[6,12,192]{2,1,0:T(8,128)S(1)}, f32[6,12,192]{2,1,0:T(8,128)}, u32[]{:S(2)}) copy-start(f32[6,12,192]{2,1,0:T(8,128)} %add_add_fusion) | copy-start | bytes 165892
  67.9 6.5 %collective-permute-start.6 = (f32[5,1,12,192]{3,1,2,0:T(1,128)S(1)}, f32[5,1,12,192]{3,1,2,0:T(1,128)S(1)}, u32[]{:S(2)}, u32[]{:S(2)}) collective-permute-start(f32[5,1,12,192]{3,1,2,0:T(1,128)S(1)} %get-tuple-element.21), channel_id=1, source_target_pairs={{16,0},{17,1},{18,2},{19,3},{20,4},{21,5},{22,6},{23,7},{24,8},{25... | collective-permute-start | bytes 138248 | tf_op jit(solution)/shard_map/ppermute | solution.py:25
  69.2 6.4 %collective-permute-start.7 = (f32[5,1,12,192]{3,1,2,0:T(1,128)S(1)}, f32[5,1,12,192]{3,1,2,0:T(1,128)S(1)}, u32[]{:S(2)}, u32[]{:S(2)}) collective-permute-start(f32[5,1,12,192]{3,1,2,0:T(1,128)S(1)} %get-tuple-element.20), channel_id=1, source_target_pairs={{0,16},{1,17},{2,18},{3,19},{4,20},{5,21},{6,22},{7,23},{8,24},{9,... | collective-permute-start | bytes 138248 | tf_op jit(solution)/shard_map/ppermute | solution.py:24
  75.6 5.4 %collective-permute-start.8 = (f32[5,8,1,192]{3,1,2,0:T(8,128)S(1)}, f32[5,8,1,192]{3,1,2,0:T(8,128)S(1)}, u32[]{:S(2)}, u32[]{:S(2)}) collective-permute-start(f32[5,8,1,192]{3,1,2,0:T(8,128)S(1)} %get-tuple-element.13), channel_id=1, source_target_pairs={{4,0},{8,4},{12,8},{5,1},{9,5},{13,9},{6,2},{10,6},{14,10},{7,3},{... | collective-permute-start | bytes 92168 | tf_op jit(solution)/shard_map/ppermute | solution.py:25
  76.9 4.1 %collective-permute-start.9 = (f32[5,8,1,192]{3,1,2,0:T(8,128)S(1)}, f32[5,8,1,192]{3,1,2,0:T(8,128)S(1)}, u32[]{:S(2)}, u32[]{:S(2)}) collective-permute-start(f32[5,8,1,192]{3,1,2,0:T(8,128)S(1)} %get-tuple-element.12), channel_id=1, source_target_pairs={{0,4},{4,8},{8,12},{1,5},{5,9},{9,13},{2,6},{6,10},{10,14},{3,7},{... | collective-permute-start | bytes 92168 | tf_op jit(solution)/shard_map/ppermute | solution.py:24
  81.4 7.4 %collective-permute-start.11 = (f32[5,8,14,1]{3,1,2,0:T(8,128)S(1)}, f32[5,8,14,1]{3,1,2,0:T(8,128)S(1)}, u32[]{:S(2)}, u32[]{:S(2)}) collective-permute-start(f32[5,8,14,1]{3,1,2,0:T(8,128)S(1)} %get-tuple-element.17), channel_id=1, source_target_pairs={{0,1},{1,2},{2,3},{4,5},{5,6},{6,7},{8,9},{9,10},{10,11},{12,13},{... | collective-permute-start | bytes 6728 | tf_op jit(solution)/shard_map/ppermute | solution.py:24
  83.8 9.7 %collective-permute-start.10 = (f32[5,8,14,1]{3,1,2,0:T(8,128)S(1)}, f32[5,8,14,1]{3,1,2,0:T(8,128)S(1)}, u32[]{:S(2)}, u32[]{:S(2)}) collective-permute-start(f32[5,8,14,1]{3,1,2,0:T(8,128)S(1)} %get-tuple-element.16), channel_id=1, source_target_pairs={{1,0},{2,1},{3,2},{5,4},{6,5},{7,6},{9,8},{10,9},{11,10},{13,12},{... | collective-permute-start | bytes 6728 | tf_op jit(solution)/shard_map/ppermute | solution.py:25
  97.4 17.9 %copy-start.5 = (f32[64,128]{1,0:T(8,128)S(1)}, f32[64,128]{1,0:T(8,128)}, u32[]{:S(2)}) copy-start(f32[64,128]{1,0:T(8,128)} %get-tuple-element.27) | copy-start | bytes 98308
  97.4 17.9 %copy-start.6 = (f32[64,128]{1,0:T(8,128)S(1)}, f32[64,128]{1,0:T(8,128)}, u32[]{:S(2)}) copy-start(f32[64,128]{1,0:T(8,128)} %get-tuple-element.28) | copy-start | bytes 98308
  97.4 17.9 %copy-start.7 = (f32[64,128]{1,0:T(8,128)S(1)}, f32[64,128]{1,0:T(8,128)}, u32[]{:S(2)}) copy-start(f32[64,128]{1,0:T(8,128)} %get-tuple-element.30) | copy-start | bytes 98308
  97.4 17.9 %copy-start.8 = (f32[64,128]{1,0:T(8,128)S(1)}, f32[64,128]{1,0:T(8,128)}, u32[]{:S(2)}) copy-start(f32[64,128]{1,0:T(8,128)} %get-tuple-element.24) | copy-start | bytes 98308
  97.5 17.9 %copy-start.9 = (f32[64,128]{1,0:T(8,128)S(1)}, f32[64,128]{1,0:T(8,128)}, u32[]{:S(2)}) copy-start(f32[64,128]{1,0:T(8,128)} %get-tuple-element.25) | copy-start | bytes 98308
  97.5 17.9 %copy-start.10 = (f32[64,128]{1,0:T(8,128)S(1)}, f32[64,128]{1,0:T(8,128)}, u32[]{:S(2)}) copy-start(f32[64,128]{1,0:T(8,128)} %get-tuple-element.26) | copy-start | bytes 98308
where the time goes:
time: 144 us
  blocking collectives  53.4 us (37%)
  starting transfers between devices  30.3 us (21%)
  local copies, waits for them, and re-layouts  19.8 us (14%)
  matrix products  17.4 us (12%)
  waiting for transfers between devices  11.9 us (8%)
  other arithmetic  9.8 us (7%)
    psum x1, blocking collectives, on_device(): spectra = lax.psum(partial_sums, ('flow', 'col'))  25.7 us
    ppermute x6, starting transfers between devices, with_halo(): before = lax.ppermute(last, axis, up)  22.3 us
    all_gather x1, blocking collectives, on_device(): lax.all_gather(surface_samples, 'row', axis=2, tiled=True)  14.4 us
    all_gather x1, blocking collectives, on_device(): lax.all_gather(panel_points, 'row', axis=1, tiled=True)  13.2 us
    dot_general x12, matrix products, contract_small(): result = jnp.einsum('...p,qp->...q', blocked, matrix, precision=HIGH)  11.6 us
    ppermute x6, starting transfers between devices, with_halo(): after = lax.ppermute(first, axis, down)  7.92 us
    ppermute x6, waiting for transfers between devices, with_halo(): after = lax.ppermute(first, axis, down)  6.94 us
    mul x1, other arithmetic, on_device(): wide_back = jnp.kron(identity, eigen_bases[2])  4.95 us
  transfers between devices with their start and end apart: 12, of which 5 were waited for; matrix products, arithmetic and copies ran while one was open for 20% of the time, Pallas kernels for 0%

commit v1 on v0

--- a/solution.py
+++ b/solution.py
@@ -161,7 +161,8 @@
     source_re, source_im = transform(samples)
     own_obs = lax.dynamic_slice_in_dim(observers, lax.axis_index("row") * count, count, 1)
     partial_sums = far_terms(own_obs, points, source_re, source_im)
-    spectra = lax.psum(partial_sums, ("flow", "col"))
+    test_knots = lambda m: lax.psum(lax.psum(m, "col"), "flow")
+    spectra = test_knots(partial_sums)
     return (state, spectra)
 
 

time: 144 us -> 140 us (0.972)
  blocking collectives: 53.4 us -> 48.8 us
    psum x1 -> x2, blocking collectives: 25.7 us -> 21.1 us  [on_device(): test_knots = lambda m: lax.psum(lax.psum(m, 'col'), 'flow')]
where the time goes in v1:
time: 140 us; the launch traced here: 139 us
  blocking collectives  48.8 us (35%)
  starting transfers between devices  30.3 us (22%)
  local copies, waits for them, and re-layouts  19.8 us (14%)
  matrix products  17.4 us (12%)
  waiting for transfers between devices  11.8 us (8%)
  other arithmetic  9.8 us (7%)
    ppermute x6, starting transfers between devices, with_halo(): before = lax.ppermute(last, axis, up)  22.3 us
    psum x2, blocking collectives, on_device(): test_knots = lambda m: lax.psum(lax.psum(m, 'col'), 'flow')  21.1 us
    all_gather x1, blocking collectives, on_device(): lax.all_gather(surface_samples, 'row', axis=2, tiled=True)  14.5 us
    all_gather x1, blocking collectives, on_device(): lax.all_gather(panel_points, 'row', axis=1, tiled=True)  13.2 us
    dot_general x12, matrix products, contract_small(): result = jnp.einsum('...p,qp->...q', blocked, matrix, precision=HIGH)  11.6 us
    ppermute x6, starting transfers between devices, with_halo(): after = lax.ppermute(first, axis, down)  7.92 us
    ppermute x6, waiting for transfers between devices, with_halo(): after = lax.ppermute(first, axis, down)  6.94 us
    mul x1, other arithmetic, on_device(): wide_back = jnp.kron(identity, eigen_bases[2])  4.95 us
  transfers between devices with their start and end apart: 12, of which 5 were waited for; matrix products, arithmetic and copies ran while one was open for 20% of the time, Pallas kernels for 0%

profile of v1, /device:TPU:0, one launch (start us, length us, event | category | flops | bytes accessed | tf_op | source)
XLA Modules:
  0.0 139.2 jit_solution(3949858778457052444)
XLA Ops:
  0.6 0.9 fusion.168
  1.7 1.3 collective-permute-start
  3.0 4.8 %collective-permute-start.1 = (f32[5,1,12,192]{3,1,2,0:T(1,128)S(1)}, f32[5,1,12,192]{3,1,2,0:T(1,128)S(1)}, u32[]{:S(2)}, u32[]{:S(2)}) collective-permute-start(f32[5,1,12,192]{3,1,2,0:T(1,128)S(1)} %copy.139), channel_id=1, source_target_pairs={{0,16},{1,17},{2,18},{3,19},{4,20},{5,21},{6,22},{7,23},{8,24},{9,... | collective-permute-start | bytes 138248 | tf_op jit(solution)/shard_map/ppermute | solution.py:24
  7.9 1.3 copy.153
  10.8 0.9 fusion.131
  11.7 4.9 %broadcast_multiply_fusion = (f32[32,6,32,6]{3,2,1,0:T(8,128)}, f32[32,6,32,6]{3,2,1,0:T(8,128)}, f32[32,6,32,6]{3,2,1,0:T(8,128)}) fusion(f32[6,6]{1,0:T(8,128)S(1)} %get-tuple-element.42, f32[32,32]{1,0:T(8,128)S(1)} %fusion.118, f32[6,6]{1,0:T(8,128)S(1)} %copy.146, f32[6,6]{1,0:T(8,128)S(1)} %fusion.131), kind=kLoop, calls=%fused_computation | loop fusion | flops 110592 | bytes 446896 | tf_op jit(solution)/shard_map/jit(kron)/mul | solution.py:114
  16.6 3.9 %reshape.301 = f32[192,192,1,1]{1,0,2,3:T(8,128)S(1)} reshape(f32[32,6,32,6]{3,2,1,0:T(8,128)} %get-tuple-element.41) | data formatting | bytes 294912 | tf_op jit(solution)/shard_map/jit(kron)/mul | solution.py:112
  22.9 13.2 %all-gather = f32[4,32,3]{1,2,0:T(4,128)S(1)} all-gather(f32[1,32,3]{1,2,0:T(4,128)S(1)} %bitcast.282), channel_id=1, replica_groups=mesh['flow'=2,'col'=4,'row'=4] {'row'}, dimensions={0}, use_global_device_ids=true | all-gather | bytes 1920 | tf_op jit(solution)/shard_map/all_gather | solution.py:158
  38.5 1.1 fusion.3
  39.7 1.3 collective-permute-start.2
  41.0 3.0 %collective-permute-start.3 = (f32[5,8,1,192]{3,1,2,0:T(8,128)S(1)}, f32[5,8,1,192]{3,1,2,0:T(8,128)S(1)}, u32[]{:S(2)}, u32[]{:S(2)}) collective-permute-start(f32[5,8,1,192]{3,1,2,0:T(8,128)S(1)} %get-tuple-element.14), channel_id=1, source_target_pairs={{0,4},{4,8},{8,12},{1,5},{5,9},{9,13},{2,6},{6,10},{10,14},{3,7},{... | collective-permute-start | bytes 92168 | tf_op jit(solution)/shard_map/ppermute | solution.py:24
  45.2 4.2 %collective-permute-start.5 = (f32[5,8,14,1]{3,1,2,0:T(8,128)S(1)}, f32[5,8,14,1]{3,1,2,0:T(8,128)}, u32[]{:S(2)}, u32[]{:S(2)}) collective-permute-start(f32[5,8,14,1]{3,1,2,0:T(8,128)S(1)} %get-tuple-element.19), channel_id=1, source_target_pairs={{0,1},{1,2},{2,3},{4,5},{5,6},{6,7},{8,9},{9,10},{10,11},{12,13},{... | collective-permute-start | bytes 6728 | tf_op jit(solution)/shard_map/ppermute | solution.py:24
  49.5 1.5 %collective-permute-start.4 = (f32[5,8,14,1]{3,1,2,0:T(8,128)S(1)}, f32[5,8,14,1]{3,1,2,0:T(8,128)}, u32[]{:S(2)}, u32[]{:S(2)}) collective-permute-start(f32[5,8,14,1]{3,1,2,0:T(8,128)S(1)} %get-tuple-element.18), channel_id=1, source_target_pairs={{1,0},{2,1},{3,2},{5,4},{6,5},{7,6},{9,8},{10,9},{11,10},{13,12},{... | collective-permute-start | bytes 6728 | tf_op jit(solution)/shard_map/ppermute | solution.py:25
  50.9 3.9 %reshape.304 = f32[192,192,1,1]{1,0,2,3:T(8,128)S(1)} reshape(f32[32,6,32,6]{3,2,1,0:T(8,128)} %get-tuple-element.40) | data formatting | bytes 294912 | tf_op jit(solution)/shard_map/jit(kron)/mul | solution.py:113
  54.8 3.9 %reshape.307 = f32[192,192,1,1]{1,0,2,3:T(8,128)S(1)} reshape(f32[32,6,32,6]{3,2,1,0:T(8,128)} %get-tuple-element.39) | data formatting | bytes 294912 | tf_op jit(solution)/shard_map/jit(kron)/mul | solution.py:114
  58.8 2.2 %collective-permute-done.4 = f32[5,8,14,1]{3,1,2,0:T(8,128)} collective-permute-done((f32[5,8,14,1]{3,1,2,0:T(8,128)S(1)}, f32[5,8,14,1]{3,1,2,0:T(8,128)}, u32[]{:S(2)}, u32[]{:S(2)}) %collective-permute-start.4) | collective-permute-done | bytes 2272 | tf_op jit(solution)/shard_map/ppermute | solution.py:25
  61.0 2.7 %fusion.55 = f32[5,12,192,6]{2,3,1,0:T(8,128)S(1)} fusion(f32[5,6,12,192]{3,1,2,0:T(8,128)S(1)} %fusion.3, f32[5,8,14,1]{3,1,2,0:T(8,128)} %collective-permute-done.5, f32[5,8,1,192]{3,1,2,0:T(8,128)S(1)} %collective-permute-done.2, f32[5,8,1,192]{3,1,2,0:T(8,128)S(1)} %collective-permute-done.3, f32[5,1,12,192]{3,1,2,0:T(1,128)S(1)} %collective-permute-done, ...), kind=kOutput, calls=%fused_computation.96 | convolution fusion | flops 7119360 | bytes 1476992 | tf_op jit(solution)/shard_map/...p,qp->...q/dot_general | solution.py:35
  67.9 1.3 collective-permute-start.6
  69.2 4.5 %collective-permute-start.7 = (f32[5,1,12,192]{3,1,2,0:T(1,128)S(1)}, f32[5,1,12,192]{3,1,2,0:T(1,128)S(1)}, u32[]{:S(2)}, u32[]{:S(2)}) collective-permute-start(f32[5,1,12,192]{3,1,2,0:T(1,128)S(1)} %get-tuple-element.20), channel_id=1, source_target_pairs={{0,16},{1,17},{2,18},{3,19},{4,20},{5,21},{6,22},{7,23},{8,24},{9,... | collective-permute-start | bytes 138248 | tf_op jit(solution)/shard_map/ppermute | solution.py:24
  74.4 1.2 collective-permute-done.7
  75.6 1.3 collective-permute-start.8
  76.9 3.3 %collective-permute-start.9 = (f32[5,8,1,192]{3,1,2,0:T(8,128)S(1)}, f32[5,8,1,192]{3,1,2,0:T(8,128)S(1)}, u32[]{:S(2)}, u32[]{:S(2)}) collective-permute-start(f32[5,8,1,192]{3,1,2,0:T(8,128)S(1)} %get-tuple-element.12), channel_id=1, source_target_pairs={{0,4},{4,8},{8,12},{1,5},{5,9},{9,13},{2,6},{6,10},{10,14},{3,7},{... | collective-permute-start | bytes 92168 | tf_op jit(solution)/shard_map/ppermute | solution.py:24
  81.4 2.4 %collective-permute-start.11 = (f32[5,8,14,1]{3,1,2,0:T(8,128)S(1)}, f32[5,8,14,1]{3,1,2,0:T(8,128)S(1)}, u32[]{:S(2)}, u32[]{:S(2)}) collective-permute-start(f32[5,8,14,1]{3,1,2,0:T(8,128)S(1)} %get-tuple-element.17), channel_id=1, source_target_pairs={{0,1},{1,2},{2,3},{4,5},{5,6},{6,7},{8,9},{9,10},{10,11},{12,13},{... | collective-permute-start | bytes 6728 | tf_op jit(solution)/shard_map/ppermute | solution.py:24
  83.8 1.3 collective-permute-start.10
  85.9 2.9 %collective-permute-done.11 = f32[5,8,14,1]{3,1,2,0:T(8,128)S(1)} collective-permute-done((f32[5,8,14,1]{3,1,2,0:T(8,128)S(1)}, f32[5,8,14,1]{3,1,2,0:T(8,128)S(1)}, u32[]{:S(2)}, u32[]{:S(2)}) %collective-permute-start.11) | collective-permute-done | bytes 2272 | tf_op jit(solution)/shard_map/ppermute | solution.py:24
  88.8 4.7 %collective-permute-done.10 = f32[5,8,14,1]{3,1,2,0:T(8,128)S(1)} collective-permute-done((f32[5,8,14,1]{3,1,2,0:T(8,128)S(1)}, f32[5,8,14,1]{3,1,2,0:T(8,128)S(1)}, u32[]{:S(2)}, u32[]{:S(2)}) %collective-permute-start.10) | collective-permute-done | bytes 2272 | tf_op jit(solution)/shard_map/ppermute | solution.py:25
  93.5 1.7 %fusion.28 = f32[5,12,192,6]{2,3,1,0:T(8,128)S(1)} fusion(f32[5,6,12,192]{3,1,2,0:T(8,128)S(1)} %fusion.7, f32[5,8,14,1]{3,1,2,0:T(8,128)S(1)} %collective-permute-done.11, f32[5,8,1,192]{3,1,2,0:T(8,128)S(1)} %collective-permute-done.8, f32[5,8,1,192]{3,1,2,0:T(8,128)S(1)} %collective-permute-done.9, f32[5,1,12,192]{3,1,2,0:T(1,128)S(1)} %collective-permute-done.6, ...), kind=kOutput, calls=%fused_computation.57 | convolution fusion | flops 7119360 | bytes 2045952 | tf_op jit(solution)/shard_map/...p,qp->...q/dot_general | solution.py:35
  99.0 0.9 copy.174
  100.1 14.5 %all_gather.7 = f32[4,16,128]{1,0,2:T(4,128)S(1)} all-gather(f32[4,16,32]{1,0,2:T(4,128)S(1)} %pad_maximum_fusion.62), channel_id=1, replica_groups=mesh['flow'=2,'col'=4,'row'=4] {'row'}, dimensions={2}, use_global_device_ids=true | all-gather | bytes 40960 | tf_op jit(solution)/shard_map/all_gather | solution.py:159
  115.3 2.7 %fusion.17 = (f32[16,64]{1,0:T(8,128)S(1)}, f32[16,64]{1,0:T(8,128)S(1)}) fusion(f32[16,128]{1,0:T(8,128)S(1)} %get-tuple-element.36, f32[64,128]{1,0:T(8,128)S(1)} %copy-done.6, f32[64,128]{1,0:T(8,128)S(1)} %copy-done.7, f32[16,128]{1,0:T(8,128)S(1)} %get-tuple-element.37, f32[16,128]{1,0:T(8,128)S(1)} %get-tuple-element.38, ...), kind=kLoop, calls=%fused_computation.41 | loop fusion | flops 3799040 | bytes 303232 | tf_op jit(solution)/shard_map/reduce_sum | solution.py:76
  118.1 11.5 %psum.14 = f32[2,16,64]{2,1,0:T(8,128)S(1)} all-reduce(f32[2,16,64]{2,1,0:T(8,128)S(1)} %pad_maximum_fusion.69), channel_id=1, replica_groups=mesh['flow'=2,'col'=4,'row'=4] {'col'}, use_global_device_ids=true, to_apply=%region_3.4 | all-reduce | flops 2048 | bytes 16384 | tf_op jit(solution)/shard_map/psum | solution.py:164
  129.6 9.6 %psum.15 = f32[2,16,64]{2,1,0:T(8,128)} all-reduce(f32[2,16,64]{2,1,0:T(8,128)S(1)} %psum.14), channel_id=1, replica_groups=mesh['flow'=2,'col'=4,'row'=4] {'flow'}, use_global_device_ids=true, to_apply=%region_4.5 | all-reduce | flops 2048 | bytes 16384 | tf_op jit(solution)/shard_map/psum | solution.py:164
  (103 shorter events, 19.0 us)
Async XLA Ops:
  0.6 35.6 %copy-start = (f32[3,256]{1,0:T(4,128)S(1)}, f32[3,256]{1,0:T(4,128)}, u32[]{:S(2)}) copy-start(f32[3,256]{1,0:T(4,128)} %param.13) | copy-start | bytes 9220
  1.7 38.0 %collective-permute-start = (f32[5,1,12,192]{3,1,2,0:T(1,128)S(1)}, f32[5,1,12,192]{3,1,2,0:T(1,128)S(1)}, u32[]{:S(2)}, u32[]{:S(2)}) collective-permute-start(f32[5,1,12,192]{3,1,2,0:T(1,128)S(1)} %copy.137), channel_id=1, source_target_pairs={{16,0},{17,1},{18,2},{19,3},{20,4},{21,5},{22,6},{23,7},{24,8},{25... | collective-permute-start | bytes 138248 | tf_op jit(solution)/shard_map/ppermute | solution.py:25
  3.0 36.6 %collective-permute-start.1 = (f32[5,1,12,192]{3,1,2,0:T(1,128)S(1)}, f32[5,1,12,192]{3,1,2,0:T(1,128)S(1)}, u32[]{:S(2)}, u32[]{:S(2)}) collective-permute-start(f32[5,1,12,192]{3,1,2,0:T(1,128)S(1)} %copy.139), channel_id=1, source_target_pairs={{0,16},{1,17},{2,18},{3,19},{4,20},{5,21},{6,22},{7,23},{8,24},{9,... | collective-permute-start | bytes 138248 | tf_op jit(solution)/shard_map/ppermute | solution.py:24
  16.6 4.0 %copy-start.1 = (f32[5,6,12,192]{3,2,1,0:T(8,128)S(1)}, f32[5,6,12,192]{3,2,1,0:T(8,128)}, u32[]{:S(2)}) copy-start(f32[5,6,12,192]{3,2,1,0:T(8,128)} %param.9) | copy-start | bytes 829444
  16.6 4.7 %copy-start.3 = (f32[3,6,6]{2,1,0:T(8,128)S(1)}, f32[3,6,6]{2,1,0:T(8,128)}, u32[]{:S(2)}) copy-start(f32[3,6,6]{2,1,0:T(8,128)} %param.11) | copy-start | bytes 1300
  16.6 5.8 %copy-start.13 = (f32[1,2,32]{2,1,0:T(2,128)S(1)}, f32[1,2,32]{2,1,0:T(2,128)}, u32[]{:S(2)}) copy-start(f32[1,2,32]{2,1,0:T(2,128)} %param.10) | copy-start | bytes 772
  16.6 6.3 %copy-start.12 = (f32[3,32]{1,0:T(4,128)S(1)}, f32[3,32]{1,0:T(4,128)}, u32[]{:S(2)}) copy-start(f32[3,32]{1,0:T(4,128)} %param.14) | copy-start | bytes 1156
  16.6 21.9 %copy-start.2 = (f32[5,6,12,192]{3,2,1,0:T(8,128)S(1)}, f32[5,6,12,192]{3,2,1,0:T(8,128)}, u32[]{:S(2)}) copy-start(f32[5,6,12,192]{3,2,1,0:T(8,128)} %param.8) | copy-start | bytes 829444
  39.7 4.4 %collective-permute-start.2 = (f32[5,8,1,192]{3,1,2,0:T(8,128)S(1)}, f32[5,8,1,192]{3,1,2,0:T(8,128)S(1)}, u32[]{:S(2)}, u32[]{:S(2)}) collective-permute-start(f32[5,8,1,192]{3,1,2,0:T(8,128)S(1)} %get-tuple-element.15), channel_id=1, source_target_pairs={{4,0},{8,4},{12,8},{5,1},{9,5},{13,9},{6,2},{10,6},{14,10},{7,3},{... | collective-permute-start | bytes 92168 | tf_op jit(solution)/shard_map/ppermute | solution.py:25
  41.0 3.9 %collective-permute-start.3 = (f32[5,8,1,192]{3,1,2,0:T(8,128)S(1)}, f32[5,8,1,192]{3,1,2,0:T(8,128)S(1)}, u32[]{:S(2)}, u32[]{:S(2)}) collective-permute-start(f32[5,8,1,192]{3,1,2,0:T(8,128)S(1)} %get-tuple-element.14), channel_id=1, source_target_pairs={{0,4},{4,8},{8,12},{1,5},{5,9},{9,13},{2,6},{6,10},{10,14},{3,7},{... | collective-permute-start | bytes 92168 | tf_op jit(solution)/shard_map/ppermute | solution.py:24
  45.2 13.5 %collective-permute-start.5 = (f32[5,8,14,1]{3,1,2,0:T(8,128)S(1)}, f32[5,8,14,1]{3,1,2,0:T(8,128)}, u32[]{:S(2)}, u32[]{:S(2)}) collective-permute-start(f32[5,8,14,1]{3,1,2,0:T(8,128)S(1)} %get-tuple-element.19), channel_id=1, source_target_pairs={{0,1},{1,2},{2,3},{4,5},{5,6},{6,7},{8,9},{9,10},{10,11},{12,13},{... | collective-permute-start | bytes 6728 | tf_op jit(solution)/shard_map/ppermute | solution.py:24
  49.5 11.6 %collective-permute-start.4 = (f32[5,8,14,1]{3,1,2,0:T(8,128)S(1)}, f32[5,8,14,1]{3,1,2,0:T(8,128)}, u32[]{:S(2)}, u32[]{:S(2)}) collective-permute-start(f32[5,8,14,1]{3,1,2,0:T(8,128)S(1)} %get-tuple-element.18), channel_id=1, source_target_pairs={{1,0},{2,1},{3,2},{5,4},{6,5},{7,6},{9,8},{10,9},{11,10},{13,12},{... | collective-permute-start | bytes 6728 | tf_op jit(solution)/shard_map/ppermute | solution.py:25
  50.9 7.7 %copy-start.11 = (f32[4,15,32]{2,0,1:T(4,128)S(1)}, f32[4,15,32]{2,0,1:T(4,128)}, u32[]{:S(2)}) copy-start(f32[4,15,32]{2,0,1:T(4,128)} %param.15) | copy-start | bytes 23044
  61.0 3.6 %copy-start.4 = (f32[6,12,192]{2,1,0:T(8,128)S(1)}, f32[6,12,192]{2,1,0:T(8,128)}, u32[]{:S(2)}) copy-start(f32[6,12,192]{2,1,0:T(8,128)} %add_add_fusion) | copy-start | bytes 165892
  67.9 6.5 %collective-permute-start.6 = (f32[5,1,12,192]{3,1,2,0:T(1,128)S(1)}, f32[5,1,12,192]{3,1,2,0:T(1,128)S(1)}, u32[]{:S(2)}, u32[]{:S(2)}) collective-permute-start(f32[5,1,12,192]{3,1,2,0:T(1,128)S(1)} %get-tuple-element.21), channel_id=1, source_target_pairs={{16,0},{17,1},{18,2},{19,3},{20,4},{21,5},{22,6},{23,7},{24,8},{25... | collective-permute-start | bytes 138248 | tf_op jit(solution)/shard_map/ppermute | solution.py:25
  69.2 6.4 %collective-permute-start.7 = (f32[5,1,12,192]{3,1,2,0:T(1,128)S(1)}, f32[5,1,12,192]{3,1,2,0:T(1,128)S(1)}, u32[]{:S(2)}, u32[]{:S(2)}) collective-permute-start(f32[5,1,12,192]{3,1,2,0:T(1,128)S(1)} %get-tuple-element.20), channel_id=1, source_target_pairs={{0,16},{1,17},{2,18},{3,19},{4,20},{5,21},{6,22},{7,23},{8,24},{9,... | collective-permute-start | bytes 138248 | tf_op jit(solution)/shard_map/ppermute | solution.py:24
  75.6 5.4 %collective-permute-start.8 = (f32[5,8,1,192]{3,1,2,0:T(8,128)S(1)}, f32[5,8,1,192]{3,1,2,0:T(8,128)S(1)}, u32[]{:S(2)}, u32[]{:S(2)}) collective-permute-start(f32[5,8,1,192]{3,1,2,0:T(8,128)S(1)} %get-tuple-element.13), channel_id=1, source_target_pairs={{4,0},{8,4},{12,8},{5,1},{9,5},{13,9},{6,2},{10,6},{14,10},{7,3},{... | collective-permute-start | bytes 92168 | tf_op jit(solution)/shard_map/ppermute | solution.py:25
  76.9 4.1 %collective-permute-start.9 = (f32[5,8,1,192]{3,1,2,0:T(8,128)S(1)}, f32[5,8,1,192]{3,1,2,0:T(8,128)S(1)}, u32[]{:S(2)}, u32[]{:S(2)}) collective-permute-start(f32[5,8,1,192]{3,1,2,0:T(8,128)S(1)} %get-tuple-element.12), channel_id=1, source_target_pairs={{0,4},{4,8},{8,12},{1,5},{5,9},{9,13},{2,6},{6,10},{10,14},{3,7},{... | collective-permute-start | bytes 92168 | tf_op jit(solution)/shard_map/ppermute | solution.py:24
  81.4 7.4 %collective-permute-start.11 = (f32[5,8,14,1]{3,1,2,0:T(8,128)S(1)}, f32[5,8,14,1]{3,1,2,0:T(8,128)S(1)}, u32[]{:S(2)}, u32[]{:S(2)}) collective-permute-start(f32[5,8,14,1]{3,1,2,0:T(8,128)S(1)} %get-tuple-element.17), channel_id=1, source_target_pairs={{0,1},{1,2},{2,3},{4,5},{5,6},{6,7},{8,9},{9,10},{10,11},{12,13},{... | collective-permute-start | bytes 6728 | tf_op jit(solution)/shard_map/ppermute | solution.py:24
  83.8 9.7 %collective-permute-start.10 = (f32[5,8,14,1]{3,1,2,0:T(8,128)S(1)}, f32[5,8,14,1]{3,1,2,0:T(8,128)S(1)}, u32[]{:S(2)}, u32[]{:S(2)}) collective-permute-start(f32[5,8,14,1]{3,1,2,0:T(8,128)S(1)} %get-tuple-element.16), channel_id=1, source_target_pairs={{1,0},{2,1},{3,2},{5,4},{6,5},{7,6},{9,8},{10,9},{11,10},{13,12},{... | collective-permute-start | bytes 6728 | tf_op jit(solution)/shard_map/ppermute | solution.py:25
  97.4 17.9 %copy-start.5 = (f32[64,128]{1,0:T(8,128)S(1)}, f32[64,128]{1,0:T(8,128)}, u32[]{:S(2)}) copy-start(f32[64,128]{1,0:T(8,128)} %get-tuple-element.27) | copy-start | bytes 98308
  97.4 17.9 %copy-start.6 = (f32[64,128]{1,0:T(8,128)S(1)}, f32[64,128]{1,0:T(8,128)}, u32[]{:S(2)}) copy-start(f32[64,128]{1,0:T(8,128)} %get-tuple-element.28) | copy-start | bytes 98308
  97.4 17.9 %copy-start.7 = (f32[64,128]{1,0:T(8,128)S(1)}, f32[64,128]{1,0:T(8,128)}, u32[]{:S(2)}) copy-start(f32[64,128]{1,0:T(8,128)} %get-tuple-element.30) | copy-start | bytes 98308
  97.4 17.9 %copy-start.8 = (f32[64,128]{1,0:T(8,128)S(1)}, f32[64,128]{1,0:T(8,128)}, u32[]{:S(2)}) copy-start(f32[64,128]{1,0:T(8,128)} %get-tuple-element.24) | copy-start | bytes 98308
  97.4 17.9 %copy-start.9 = (f32[64,128]{1,0:T(8,128)S(1)}, f32[64,128]{1,0:T(8,128)}, u32[]{:S(2)}) copy-start(f32[64,128]{1,0:T(8,128)} %get-tuple-element.25) | copy-start | bytes 98308
  97.4 17.9 %copy-start.10 = (f32[64,128]{1,0:T(8,128)S(1)}, f32[64,128]{1,0:T(8,128)}, u32[]{:S(2)}) copy-start(f32[64,128]{1,0:T(8,128)} %get-tuple-element.26) | copy-start | bytes 98308
